TPU v7x, 32 devices: a whole 2x2x4 slice. The times are simulated.
32 devices in a mesh: seq: 8 (over z, x), head: 4 (over y, core).
Axes of the slice: x: 2, y: 2, z: 4, core: 2. Of those that a mesh axis runs over, the one named last changes fastest.
Arguments:
- queries: bfloat16 [16384, 2048], P(('seq', 'head')), may hold values from -6 to 6
- keys: bfloat16 [16384, 2048], P(('seq', 'head')), may hold values from -6 to 6
- values: bfloat16 [16384, 2048], P(('seq', 'head')), may hold values from -44.2 to 44.2
- log_decay: float32 [16384, 8], P('seq', 'head'), may hold values from -0.7 to 0
- selection: int32 [4, 3], replicated, may hold values from 0 to 3, as said below
- out_gain: float32 [2048], P('head'), may hold values from 0.5 to 1.5
Outputs:
- mixed: bfloat16 [16384, 2048], P('seq', 'head')
Inputs may be any that keep to these rules, and one draw needn't show every extreme that they name: `selection`: row i begins with i; its other two entries are two different blocks before block i, or i itself where fewer than two earlier blocks exist.
All inputs are finite; a program needn't handle non-finite values.
Results may differ from a plain program's by a relative error of at most 0.0044.
Values may be sent and summed in bfloat16 or wider, within the bound.
No kernel may reach another device: no remote copies, remote signals or barrier semaphores. Data moves between devices by JAX's collectives and lax.ppermute only.
A program may use at most 128 MiB of HBM per device.

v0:
```python
import jax
import jax.numpy as jnp
from jax import lax
from jax.sharding import PartitionSpec as P

HD = 128
BLK = 4096
TILE = 1024
CH = 128


EPSILON = 1e-06
NEGATIVE = -1e30
HIGHEST = lax.Precision.HIGHEST


def carried_in(part, axis, combine, identity):
    place = lax.axis_index(axis)
    gathered = jax.tree.map(lambda a: lax.all_gather(a, axis), part)
    state = jax.tree.map(lambda a, e: jnp.zeros_like(a) + jnp.asarray(e, a.dtype), part, identity)

    def one(turn, state):
        return combine(
            state, jax.tree.map(lambda a: lax.dynamic_index_in_dim(a, turn, 0, False), gathered)
        )

    return lax.fori_loop(0, place, one, state)


def within_spans(query_lin, key_lin, value_lin, log_decay, span):
    rows, record_entries, width = query_lin.shape
    count = rows // span
    probe_segments = query_lin.reshape(count, span, record_entries, width)
    key_spans = key_lin.reshape(count, span, record_entries, width)
    value_spans = value_lin.reshape(count, span, record_entries, width)
    running = jnp.cumsum(log_decay.reshape(count, span, record_entries), axis=1)
    by_line = jnp.transpose(running, (0, 2, 1))
    causal = jnp.arange(span)[:, None] >= jnp.arange(span)[None, :]
    stride_gap = jnp.where(causal, by_line[:, :, :, None] - by_line[:, :, None, :], 0.0)
    damping = jnp.where(causal, jnp.exp(stride_gap), 0.0)
    scores = jnp.einsum(
        "ctld,csld->clts", probe_segments, key_spans, preferred_element_type=jnp.float32
    )
    mixing = (scores * damping).astype(jnp.bfloat16)
    inside = jnp.einsum("clts,csld->ctld", mixing, value_spans, preferred_element_type=jnp.float32)
    ending = running[:, -1, :]
    weighted_keys = (
        key_spans.astype(jnp.float32) * jnp.exp(ending[:, None, :] - running)[..., None]
    ).astype(jnp.bfloat16)
    increments = jnp.einsum(
        "ctld,ctle->clde", weighted_keys, value_spans, preferred_element_type=jnp.float32
    )

    def advance(state, inputs):
        decay_sum, increment = inputs
        return (jnp.exp(decay_sum)[:, None, None] * state + increment, state)

    final_state, entering = lax.scan(
        advance, jnp.zeros((record_entries, width, width), jnp.float32), (ending, increments)
    )
    weighted_queries = probe_segments.astype(jnp.float32) * jnp.exp(running)[..., None]
    across = jnp.einsum("ctld,clde->ctle", weighted_queries, entering, precision=HIGHEST)
    return (inside + across, weighted_queries, ending, final_state)


def attend_tiles(query, key_tiles, payload_blocks, query_pos, slot_open, per_slot):
    rows, record_entries, width = query.shape
    tile_len = key_tiles.shape[1]
    scale = width ** (-0.5)

    def tile_step(tile, carry):
        best, total, accum = carry
        slot = tile // per_slot
        key_pos = tile % per_slot * tile_len + jnp.arange(tile_len)
        key_tile = lax.dynamic_index_in_dim(key_tiles, tile, 0, keepdims=False)
        value_tile = lax.dynamic_index_in_dim(payload_blocks, tile, 0, keepdims=False)
        causal = key_pos[None, :] <= query_pos[:, None]
        allowed = jnp.where(slot == 0, causal, slot_open[slot])
        scores = (
            jnp.einsum("ild,jld->lij", query, key_tile, preferred_element_type=jnp.float32) * scale
        )
        masked = jnp.where(allowed[None], scores, NEGATIVE)
        tile_max = jnp.max(masked, axis=2)
        probs = jnp.where(allowed[None], jnp.exp(masked - tile_max[:, :, None]), 0.0).astype(
            jnp.bfloat16
        )
        tile_sum = jnp.sum(probs, axis=2, dtype=jnp.float32)
        tile_out = jnp.einsum("lij,jld->ild", probs, value_tile, preferred_element_type=jnp.float32)
        peak = jnp.maximum(best, tile_max)
        keep = jnp.exp(best - peak)
        fresh = jnp.exp(tile_max - peak)
        total = total * keep + tile_sum * fresh
        accum = accum * keep.T[:, :, None] + tile_out * fresh.T[:, :, None]
        return (peak, total, accum)

    start = (
        jnp.full((record_entries, rows), NEGATIVE, jnp.float32),
        jnp.zeros((record_entries, rows), jnp.float32),
        jnp.zeros((rows, record_entries, width), jnp.float32),
    )
    best, total, accum = lax.fori_loop(0, key_tiles.shape[0], tile_step, start)
    return accum / total.T[:, :, None]


def request_table(selection, group, seq_count):
    dest_block = jnp.arange(seq_count) // group
    chosen = jnp.take(selection, dest_block, axis=0)
    return jnp.transpose(chosen)[:, None, :] * group + jnp.arange(group)[None, :, None]


def normalize(heads):
    return heads * lax.rsqrt(jnp.mean(heads * heads, axis=-1, keepdims=True) + EPSILON)


def per_device(queries, keys, values, log_decay, selection, out_gain):
    queries, keys, values = (
        lax.all_to_all(queries, "head", split_axis=1, concat_axis=0, tiled=True),
        lax.all_to_all(keys, "head", split_axis=1, concat_axis=0, tiled=True),
        lax.all_to_all(values, "head", split_axis=1, concat_axis=0, tiled=True),
    )
    rows = queries.shape[0]
    width = HD
    pairs = queries.shape[1] // (2 * width)
    query_pairs = queries.reshape(rows, pairs, 2, width)
    paired_keys = keys.reshape(rows, pairs, 2, width)
    paired_values = values.reshape(rows, pairs, 2, width)
    linear_part, weighted_queries, ending, final_state = within_spans(
        query_pairs[:, :, 0], paired_keys[:, :, 0], paired_values[:, :, 0], log_decay, CH
    )
    total_decay = jnp.sum(ending, axis=0)

    def chain(earlier, later):
        return (earlier[0] + later[0], jnp.exp(later[0])[:, None, None] * earlier[1] + later[1])

    leading_decay, carried = carried_in(
        (total_decay, final_state),
        "seq",
        chain,
        (jnp.zeros_like(total_decay), jnp.zeros_like(final_state)),
    )
    span_start = jnp.cumsum(ending, axis=0) - ending
    shifted = weighted_queries * jnp.exp(span_start)[:, None, :, None]
    correction = jnp.einsum("ctld,lde->ctle", shifted, carried, precision=HIGHEST)
    linear_out = (linear_part + correction).reshape(rows, pairs, width)
    seq_count = lax.axis_size("seq")
    position = lax.axis_index("seq")
    group = BLK // rows
    block_index = position // group
    rank = position % group
    piece_rows = rows // seq_count
    query_moba = query_pairs[:, :, 1]
    key_moba = paired_keys[:, :, 1]
    value_moba = paired_values[:, :, 1]
    spread_keys, spread_values = (
        lax.all_to_all(
            key_moba.reshape(seq_count, piece_rows, pairs, width),
            "seq",
            split_axis=0,
            concat_axis=0,
            tiled=True,
        ),
        lax.all_to_all(
            value_moba.reshape(seq_count, piece_rows, pairs, width),
            "seq",
            split_axis=0,
            concat_axis=0,
            tiled=True,
        ),
    )
    table = request_table(selection, group, seq_count)
    block_keys, block_values = (
        lax.all_to_all(
            jnp.take(spread_keys, table, axis=0), "seq", split_axis=2, concat_axis=2, tiled=True
        ),
        lax.all_to_all(
            jnp.take(spread_values, table, axis=0), "seq", split_axis=2, concat_axis=2, tiled=True
        ),
    )
    block_keys = block_keys.reshape(3, BLK, pairs, width)
    block_values = block_values.reshape(3, BLK, pairs, width)
    per_slot = BLK // TILE
    key_tiles = block_keys.reshape(3 * per_slot, TILE, pairs, width)
    payload_blocks = block_values.reshape(3 * per_slot, TILE, pairs, width)
    chosen = jnp.take(selection, block_index, axis=0)
    slot_open = jnp.concatenate([jnp.ones((1,), jnp.bool_), chosen[1:] != block_index])
    query_pos = rank * rows + jnp.arange(rows)
    attended = attend_tiles(query_moba, key_tiles, payload_blocks, query_pos, slot_open, per_slot)
    both = jnp.stack([normalize(linear_out), normalize(attended)], axis=2).reshape(
        rows, pairs * 2 * width
    )
    return (both * out_gain[None, :]).astype(jnp.bfloat16)


def solution(mesh):
    return jax.shard_map(
        per_device,
        mesh=mesh,
        in_specs=(
            P(("seq", "head"), None),
            P(("seq", "head"), None),
            P(("seq", "head"), None),
            P("seq", "head"),
            P(),
            P("head"),
        ),
        out_specs=P("seq", "head"),
        check_vma=False,
    )
```

profile of v0, /device:TPU:16, one launch (start us, length us, event | category | flops | bytes accessed | tf_op | source)
XLA Modules:
  0.0 871.0 jit_solution(2189066469630119608)
XLA Ops:
  16.4 22.6 %all-to-all-done.1 = bf16[512,4,512]{2,0,1:T(8,128)(2,1)S(1)} async-done(((bf16[512,4,512]{2,0,1:T(8,128)(2,1)}), bf16[512,4,512]{2,0,1:T(8,128)(2,1)S(1)}, u32[]{:S(2)}, u32[]{:S(2)}) %all-to-all-start.1) | async-done | bytes 2097184 | tf_op jit(solution)/shard_map/all_to_all | solution.py:118
  52.3 18.1 %all-to-all-done.2 = bf16[512,4,512]{2,0,1:T(8,128)(2,1)} async-done(((bf16[512,4,512]{2,0,1:T(8,128)(2,1)}), bf16[512,4,512]{2,0,1:T(8,128)(2,1)}, u32[]{:S(2)}, u32[]{:S(2)}) %all-to-all-start.2) | async-done | bytes 2097184 | tf_op jit(solution)/shard_map/all_to_all | solution.py:119
  84.2 14.8 %all-to-all-done.3 = bf16[8,256,2,128]{3,1,2,0:T(8,128)(2,1)S(1)} async-done(((bf16[8,256,2,128]{3,1,2,0:T(8,128)(2,1)}), bf16[8,256,2,128]{3,1,2,0:T(8,128)(2,1)S(1)}, u32[]{:S(2)}, u32[]{:S(2)}) %all-to-all-start.3) | async-done | bytes 1048608 | tf_op jit(solution)/shard_map/all_to_all | solution.py:155
  109.7 18.8 %all-to-all-done.5 = bf16[8,256,2,128]{3,1,2,0:T(8,128)(2,1)S(1)} async-done(((bf16[8,256,2,128]{3,1,2,0:T(8,128)(2,1)}), bf16[8,256,2,128]{3,1,2,0:T(8,128)(2,1)S(1)}, u32[]{:S(2)}, u32[]{:S(2)}) %all-to-all-start.5) | async-done | bytes 1048608 | tf_op jit(solution)/shard_map/all_to_all | solution.py:162
  142.9 10.4 %copy_select_fusion = (bf16[3,2,8,256,2,128]{5,3,1,0,4,2:T(8,128)(2,1)}, bf16[3,2,8,256,2,128]{5,3,1,0,4,2:T(8,128)(2,1)}) fusion(bf16[3,2,8,256,2,128]{5,3,4,2,1,0:T(8,128)(2,1)} %bitcast.155, pred[3,2,8]{1,0,2:T(4,128)(4,1)S(1)} %copy.120, bf16[3,2,8,256,2,128]{5,3,4,2,1,0:T(8,128)(2,1)} %bitcast.154), kind=kLoop, calls=%fused_computation.37 | loop fusion | flops 6291456 | bytes 25165872 | tf_op jit(solution)/shard_map/jit(_take)/select_n | solution.py:176
  158.7 8.1 all-to-all-start.4
  167.3 23.3 %fusion.45 = f32[16,128,2]{2,0,1:T(8,128)S(1)} fusion(f32[16,128,2]{2,0,1:T(8,128)S(1)} %copy.100), kind=kOutput, calls=%fused_computation.104 | output fusion | flops 520192 | bytes 32768 | tf_op jit(solution)/shard_map/jit(cumsum)/reduce_window_sum | solution.py:36
  200.3 101.5 %all-to-all-done.4 = bf16[3,2,8,256,2,128]{5,3,1,0,4,2:T(8,128)(2,1)} async-done(((bf16[3,2,8,256,2,128]{5,3,1,0,4,2:T(8,128)(2,1)}), bf16[3,2,8,256,2,128]{5,3,1,0,4,2:T(8,128)(2,1)}, u32[]{:S(2)}, u32[]{:S(2)}) %all-to-all-start.4) | async-done | bytes 6291488 | tf_op jit(solution)/shard_map/all_to_all | solution.py:172
  301.7 8.1 all-to-all-start.6
  309.8 26.9 %while.50 = (s32[]{:T(128)}, f32[2,128,128]{2,1,0:T(8,128)S(1)}, f32[16,2,128,128]{3,2,1,0:T(8,128)}, f32[16,2]{1,0:T(8,128)S(1)}, f32[16,2,128,128]{3,2,1,0:T(8,128)}) while((s32[]{:T(128)}, f32[2,128,128]{2,1,0:T(8,128)S(1)}, f32[16,2,128,128]{3,2,1,0:T(8,128)}, f32[16,2]{1,0:T(8,128)S(1)}, ...), condition=%wide.region_2.3_spmd.clone.clone, body=%wide.region_1.2_spmd.clone.sunk.clone | while | flops 131075 | bytes 655976 | solution.py:58
  337.5 130.1 %all-reduce = f32[16]{0:T(128)S(1)} all-reduce(f32[16]{0:T(128)S(1)} %dynamic-update-slice.1), channel_id=2, replica_groups=mesh['seq'=8,'head'=4] {'seq'}, use_global_device_ids=true, to_apply=%add | all-reduce | flops 16 | bytes 128
  506.6 340.0 %while.51 = (s32[]{:T(128)}, f32[2,2048]{1,0:T(2,128)S(1)}, f32[2,2048]{1,0:T(2,128)S(1)}, f32[2048,2,128]{0,2,1:T(8,128)}, pred[3]{0:T(512)(128)(4,1)S(1)}, /*i...) while((s32[]{:T(128)}, f32[2,2048]{1,0:T(2,128)S(1)}, ...), condition=%wide.region_11.13_spmd.clone.clone, body=%wide.region_8.12_spmd.clone.sunk.clone | while | flops 2216725504 | bytes 132457784 | solution.py:101
  524.5 10.2 %fusion.69 = f32[2048,2,128]{0,2,1:T(8,128)} fusion(f32[2048,2,128]{0,2,1:T(8,128)} %get-tuple-element.678, f32[2048,2]{0,1:T(2,128)S(1)} %get-tuple-element.648, f32[2048,2]{0,1:T(2,128)S(1)} %get-tuple-element.649, pred[]{:T(512)S(6)} %compare.32, bf16[12,1024,2,128]{3,1,0,2:T(8,128)(2,1)} %get-tuple-element.691, s32[]{:T(128)} %get-tuple-element.675, ...), kind=kOutput, calls=%fused_computation.18.clone.1.clone | convolution fusion | flops 1096810496 | bytes 23642624 | tf_op jit(solution)/shard_map/while/body/eval_jaxpr/lij,jld->ild/dot_general | solution.py:88
  552.7 10.4 %fusion.69 = f32[2048,2,128]{0,2,1:T(8,128)} fusion(f32[2048,2,128]{0,2,1:T(8,128)} %get-tuple-element.678, f32[2048,2]{0,1:T(2,128)S(1)} %get-tuple-element.648, f32[2048,2]{0,1:T(2,128)S(1)} %get-tuple-element.649, pred[]{:T(512)S(6)} %compare.32, bf16[12,1024,2,128]{3,1,0,2:T(8,128)(2,1)} %get-tuple-element.691, s32[]{:T(128)} %get-tuple-element.675, ...), kind=kOutput, calls=%fused_computation.18.clone.1.clone | convolution fusion | flops 1096810496 | bytes 23642624 | tf_op jit(solution)/shard_map/while/body/eval_jaxpr/lij,jld->ild/dot_general | solution.py:88
  581.0 10.4 %fusion.69 = f32[2048,2,128]{0,2,1:T(8,128)} fusion(f32[2048,2,128]{0,2,1:T(8,128)} %get-tuple-element.678, f32[2048,2]{0,1:T(2,128)S(1)} %get-tuple-element.648, f32[2048,2]{0,1:T(2,128)S(1)} %get-tuple-element.649, pred[]{:T(512)S(6)} %compare.32, bf16[12,1024,2,128]{3,1,0,2:T(8,128)(2,1)} %get-tuple-element.691, s32[]{:T(128)} %get-tuple-element.675, ...), kind=kOutput, calls=%fused_computation.18.clone.1.clone | convolution fusion | flops 1096810496 | bytes 23642624 | tf_op jit(solution)/shard_map/while/body/eval_jaxpr/lij,jld->ild/dot_general | solution.py:88
  609.4 10.4 %fusion.69 = f32[2048,2,128]{0,2,1:T(8,128)} fusion(f32[2048,2,128]{0,2,1:T(8,128)} %get-tuple-element.678, f32[2048,2]{0,1:T(2,128)S(1)} %get-tuple-element.648, f32[2048,2]{0,1:T(2,128)S(1)} %get-tuple-element.649, pred[]{:T(512)S(6)} %compare.32, bf16[12,1024,2,128]{3,1,0,2:T(8,128)(2,1)} %get-tuple-element.691, s32[]{:T(128)} %get-tuple-element.675, ...), kind=kOutput, calls=%fused_computation.18.clone.1.clone | convolution fusion | flops 1096810496 | bytes 23642624 | tf_op jit(solution)/shard_map/while/body/eval_jaxpr/lij,jld->ild/dot_general | solution.py:88
  637.7 10.4 %fusion.69 = f32[2048,2,128]{0,2,1:T(8,128)} fusion(f32[2048,2,128]{0,2,1:T(8,128)} %get-tuple-element.678, f32[2048,2]{0,1:T(2,128)S(1)} %get-tuple-element.648, f32[2048,2]{0,1:T(2,128)S(1)} %get-tuple-element.649, pred[]{:T(512)S(6)} %compare.32, bf16[12,1024,2,128]{3,1,0,2:T(8,128)(2,1)} %get-tuple-element.691, s32[]{:T(128)} %get-tuple-element.675, ...), kind=kOutput, calls=%fused_computation.18.clone.1.clone | convolution fusion | flops 1096810496 | bytes 23642624 | tf_op jit(solution)/shard_map/while/body/eval_jaxpr/lij,jld->ild/dot_general | solution.py:88
  666.1 10.4 %fusion.69 = f32[2048,2,128]{0,2,1:T(8,128)} fusion(f32[2048,2,128]{0,2,1:T(8,128)} %get-tuple-element.678, f32[2048,2]{0,1:T(2,128)S(1)} %get-tuple-element.648, f32[2048,2]{0,1:T(2,128)S(1)} %get-tuple-element.649, pred[]{:T(512)S(6)} %compare.32, bf16[12,1024,2,128]{3,1,0,2:T(8,128)(2,1)} %get-tuple-element.691, s32[]{:T(128)} %get-tuple-element.675, ...), kind=kOutput, calls=%fused_computation.18.clone.1.clone | convolution fusion | flops 1096810496 | bytes 23642624 | tf_op jit(solution)/shard_map/while/body/eval_jaxpr/lij,jld->ild/dot_general | solution.py:88
  694.4 10.4 %fusion.69 = f32[2048,2,128]{0,2,1:T(8,128)} fusion(f32[2048,2,128]{0,2,1:T(8,128)} %get-tuple-element.678, f32[2048,2]{0,1:T(2,128)S(1)} %get-tuple-element.648, f32[2048,2]{0,1:T(2,128)S(1)} %get-tuple-element.649, pred[]{:T(512)S(6)} %compare.32, bf16[12,1024,2,128]{3,1,0,2:T(8,128)(2,1)} %get-tuple-element.691, s32[]{:T(128)} %get-tuple-element.675, ...), kind=kOutput, calls=%fused_computation.18.clone.1.clone | convolution fusion | flops 1096810496 | bytes 23642624 | tf_op jit(solution)/shard_map/while/body/eval_jaxpr/lij,jld->ild/dot_general | solution.py:88
  722.8 10.4 %fusion.69 = f32[2048,2,128]{0,2,1:T(8,128)} fusion(f32[2048,2,128]{0,2,1:T(8,128)} %get-tuple-element.678, f32[2048,2]{0,1:T(2,128)S(1)} %get-tuple-element.648, f32[2048,2]{0,1:T(2,128)S(1)} %get-tuple-element.649, pred[]{:T(512)S(6)} %compare.32, bf16[12,1024,2,128]{3,1,0,2:T(8,128)(2,1)} %get-tuple-element.691, s32[]{:T(128)} %get-tuple-element.675, ...), kind=kOutput, calls=%fused_computation.18.clone.1.clone | convolution fusion | flops 1096810496 | bytes 23642624 | tf_op jit(solution)/shard_map/while/body/eval_jaxpr/lij,jld->ild/dot_general | solution.py:88
  751.1 10.4 %fusion.69 = f32[2048,2,128]{0,2,1:T(8,128)} fusion(f32[2048,2,128]{0,2,1:T(8,128)} %get-tuple-element.678, f32[2048,2]{0,1:T(2,128)S(1)} %get-tuple-element.648, f32[2048,2]{0,1:T(2,128)S(1)} %get-tuple-element.649, pred[]{:T(512)S(6)} %compare.32, bf16[12,1024,2,128]{3,1,0,2:T(8,128)(2,1)} %get-tuple-element.691, s32[]{:T(128)} %get-tuple-element.675, ...), kind=kOutput, calls=%fused_computation.18.clone.1.clone | convolution fusion | flops 1096810496 | bytes 23642624 | tf_op jit(solution)/shard_map/while/body/eval_jaxpr/lij,jld->ild/dot_general | solution.py:88
  779.5 10.4 %fusion.69 = f32[2048,2,128]{0,2,1:T(8,128)} fusion(f32[2048,2,128]{0,2,1:T(8,128)} %get-tuple-element.678, f32[2048,2]{0,1:T(2,128)S(1)} %get-tuple-element.648, f32[2048,2]{0,1:T(2,128)S(1)} %get-tuple-element.649, pred[]{:T(512)S(6)} %compare.32, bf16[12,1024,2,128]{3,1,0,2:T(8,128)(2,1)} %get-tuple-element.691, s32[]{:T(128)} %get-tuple-element.675, ...), kind=kOutput, calls=%fused_computation.18.clone.1.clone | convolution fusion | flops 1096810496 | bytes 23642624 | tf_op jit(solution)/shard_map/while/body/eval_jaxpr/lij,jld->ild/dot_general | solution.py:88
  807.9 10.4 %fusion.69 = f32[2048,2,128]{0,2,1:T(8,128)} fusion(f32[2048,2,128]{0,2,1:T(8,128)} %get-tuple-element.678, f32[2048,2]{0,1:T(2,128)S(1)} %get-tuple-element.648, f32[2048,2]{0,1:T(2,128)S(1)} %get-tuple-element.649, pred[]{:T(512)S(6)} %compare.32, bf16[12,1024,2,128]{3,1,0,2:T(8,128)(2,1)} %get-tuple-element.691, s32[]{:T(128)} %get-tuple-element.675, ...), kind=kOutput, calls=%fused_computation.18.clone.1.clone | convolution fusion | flops 1096810496 | bytes 23642624 | tf_op jit(solution)/shard_map/while/body/eval_jaxpr/lij,jld->ild/dot_general | solution.py:88
  836.2 10.4 %fusion.69 = f32[2048,2,128]{0,2,1:T(8,128)} fusion(f32[2048,2,128]{0,2,1:T(8,128)} %get-tuple-element.678, f32[2048,2]{0,1:T(2,128)S(1)} %get-tuple-element.648, f32[2048,2]{0,1:T(2,128)S(1)} %get-tuple-element.649, pred[]{:T(512)S(6)} %compare.32, bf16[12,1024,2,128]{3,1,0,2:T(8,128)(2,1)} %get-tuple-element.691, s32[]{:T(128)} %get-tuple-element.675, ...), kind=kOutput, calls=%fused_computation.18.clone.1.clone | convolution fusion | flops 1096810496 | bytes 23642624 | tf_op jit(solution)/shard_map/while/body/eval_jaxpr/lij,jld->ild/dot_general | solution.py:88
  (297 shorter events, 379.1 us)
Async XLA Ops:
  9.7 29.3 %all-to-all-start.1 = ((bf16[512,4,512]{2,0,1:T(8,128)(2,1)}), bf16[512,4,512]{2,0,1:T(8,128)(2,1)S(1)}, u32[]{:S(2)}, u32[]{:S(2)}) async-start(bf16[512,4,512]{2,0,1:T(8,128)(2,1)} %bitcast.159), calls=%async_computation.1 | async-start | bytes 4194304 | tf_op jit(solution)/shard_map/all_to_all | solution.py:118
  40.3 30.2 %all-to-all-start.2 = ((bf16[512,4,512]{2,0,1:T(8,128)(2,1)}), bf16[512,4,512]{2,0,1:T(8,128)(2,1)}, u32[]{:S(2)}, u32[]{:S(2)}) async-start(bf16[512,4,512]{2,0,1:T(8,128)(2,1)} %bitcast.104), calls=%async_computation.2 | async-start | bytes 4194304 | tf_op jit(solution)/shard_map/all_to_all | solution.py:119
  70.5 28.5 %all-to-all-start.3 = ((bf16[8,256,2,128]{3,1,2,0:T(8,128)(2,1)}), bf16[8,256,2,128]{3,1,2,0:T(8,128)(2,1)S(1)}, u32[]{:S(2)}, u32[]{:S(2)}) async-start(bf16[8,256,2,128]{3,1,2,0:T(8,128)(2,1)} %copy.122), calls=%async_computation.3 | async-start | bytes 2097152 | tf_op jit(solution)/shard_map/all_to_all | solution.py:155
  99.0 29.4 %all-to-all-start.5 = ((bf16[8,256,2,128]{3,1,2,0:T(8,128)(2,1)}), bf16[8,256,2,128]{3,1,2,0:T(8,128)(2,1)S(1)}, u32[]{:S(2)}, u32[]{:S(2)}) async-start(bf16[8,256,2,128]{3,1,2,0:T(8,128)(2,1)} %copy.128), calls=%async_computation.5 | async-start | bytes 2097152 | tf_op jit(solution)/shard_map/all_to_all | solution.py:162
  128.4 30.3 %all-to-all-start = ((bf16[512,4,512]{2,0,1:T(8,128)(2,1)}), bf16[512,4,512]{2,0,1:T(8,128)(2,1)}, u32[]{:S(2)}, u32[]{:S(2)}) async-start(bf16[512,4,512]{2,0,1:T(8,128)(2,1)} %bitcast.157), calls=%async_computation | async-start | bytes 4194304 | tf_op jit(solution)/shard_map/all_to_all | solution.py:117
  158.7 8.1 copy-start.10
  158.7 143.0 %all-to-all-start.4 = ((bf16[3,2,8,256,2,128]{5,3,1,0,4,2:T(8,128)(2,1)}), bf16[3,2,8,256,2,128]{5,3,1,0,4,2:T(8,128)(2,1)}, u32[]{:S(2)}, u32[]{:S(2)}) async-start(bf16[3,2,8,256,2,128]{5,3,1,0,4,2:T(8,128)(2,1)} %get-tuple-element.473), calls=%async_computation.4 | async-start | bytes 12582912 | tf_op jit(solution)/shard_map/all_to_all | solution.py:172
  301.7 198.5 %all-to-all-start.6 = ((bf16[3,2,8,256,2,128]{5,3,1,0,4,2:T(8,128)(2,1)}), bf16[3,2,8,256,2,128]{5,3,1,0,4,2:T(8,128)(2,1)}, u32[]{:S(2)}, u32[]{:S(2)}) async-start(bf16[3,2,8,256,2,128]{5,3,1,0,4,2:T(8,128)(2,1)} %get-tuple-element.472), calls=%async_computation.6 | async-start | bytes 12582912 | tf_op jit(solution)/shard_map/all_to_all | solution.py:175
  309.8 171.7 %all-gather.4.cloned.1.call-start = ((), (), s32[]{:S(2)}) async-start(), calls=%async_computation.7 | async-start | bytes 1179648 | tf_op jit(solution)/shard_map/all_gather | solution.py:19
  485.7 3.6 copy-start.6
  500.2 6.4 copy-start.8
  514.2 5.7 copy-start
  542.3 5.7 copy-start
  570.7 5.7 copy-start
  599.0 5.7 copy-start
  627.4 5.7 copy-start
  655.8 5.7 copy-start
  684.1 5.7 copy-start
  712.5 5.7 copy-start
  740.8 5.7 copy-start
  769.2 5.7 copy-start
  797.5 5.7 copy-start
  825.9 5.7 copy-start
  853.7 5.5 copy-start.11
  (8 other events, 13.4 us)
Sparse Core Ops, SparseCore 0:
  337.6 91.4 all-gather.3
where the time goes:
time: 874 us; the launch traced here: 871 us
  matrix products  194 us (22%)
  waiting for transfers between devices  181 us (21%)
  other arithmetic  158 us (18%)
  local copies, waits for them, and re-layouts  151 us (17%)
  blocking collectives  130 us (15%)
  starting transfers between devices  41.6 us (5%)
  between operations  14.4 us (2%)
    unnamed x1, blocking collectives  130 us
    dot_general x12, matrix products, tile_step(): jnp.einsum('lij,jld->ild', probs, value_tile, preferred_element_type=jnp....  125 us
    all_to_all x1, waiting for transfers between devices, per_device(): lax.all_to_all(jnp.take(spread_keys, table, axis=0), 'seq', split_axis=2,...  101 us
    while x36, local copies, waits for them, and re-layouts  68.8 us
    dot_general x12, matrix products, tile_step(): jnp.einsum('ild,jld->lij', query, key_tile, preferred_element_type=jnp.fl...  56 us
    reduce_sum x12, other arithmetic, tile_step(): tile_sum = jnp.sum(probs, axis=2, dtype=jnp.float32)  54 us
    select_n x12, other arithmetic, tile_step(): allowed = jnp.where(slot == 0, causal, slot_open[slot])  27.7 us
    another operation x1, other arithmetic, within_spans(): running = jnp.cumsum(log_decay.reshape(count, span, record_entries), axis=1)  23.3 us
  transfers between devices with their start and end apart: 8, of which 6 were waited for; matrix products, arithmetic and copies ran while one was open for 15% of the time, Pallas kernels for 0%

commit v1 on v0

--- a/solution.py
+++ b/solution.py
@@ -1,6 +1,8 @@
 import jax
 import jax.numpy as jnp
 from jax import lax
+from jax.experimental import pallas as pl
+from jax.experimental.pallas import tpu as pltpu
 from jax.sharding import PartitionSpec as P
 
 HD = 128
@@ -12,6 +14,8 @@
 EPSILON = 1e-06
 NEGATIVE = -1e30
 HIGHEST = lax.Precision.HIGHEST
+VMEM_LIMIT = 48 << 20
+QROWS = 512
 
 
 def carried_in(part, axis, combine, identity):
@@ -191,18 +195,361 @@
     return (both * out_gain[None, :]).astype(jnp.bfloat16)
 
 
+SUB = 4
+LOG2E = 1.4426950408889634
+
+
+def dot_t(a, b):
+    return lax.dot_general(a, b, (((1,), (1,)), ((), ())), preferred_element_type=jnp.float32)
+
+
+def with_ones(v):
+    return jnp.concatenate([v, jnp.ones(v.shape, v.dtype)], axis=1)
+
+
+def own_block_kernel(q_ref, a_ref, b_ref, acc_ref, top_ref):
+    i = pl.program_id(0)
+    q = q_ref[0]
+    rows = q.shape[0]
+    scale = HD ** (-0.5) * LOG2E
+
+    def keys_of(p):
+        return jnp.concatenate([a_ref[p, 0], b_ref[p, 0]], axis=0)
+
+    def values_of(p):
+        return with_ones(jnp.concatenate([a_ref[p, 1], b_ref[p, 1]], axis=0))
+
+    s = dot_t(q, keys_of(i)) * scale
+    r = lax.broadcasted_iota(jnp.int32, s.shape, 0)
+    c = lax.broadcasted_iota(jnp.int32, s.shape, 1)
+    s = jnp.where(c <= r, s, NEGATIVE)
+    m = jnp.max(s, axis=1, keepdims=True)
+    prob = jnp.exp2(s - m).astype(jnp.bfloat16)
+    top_ref[...] = jnp.broadcast_to(m, (rows, HD))
+    acc_ref[...] = jnp.dot(prob, values_of(i), preferred_element_type=jnp.float32)
+
+    @pl.loop(0, i)
+    def _(p):
+        s = dot_t(q, keys_of(p)) * scale
+        old = top_ref[...]
+        m = jnp.maximum(old, jnp.max(s, axis=1, keepdims=True))
+        prob = jnp.exp2(s - m[:, :1]).astype(jnp.bfloat16)
+        keep = jnp.exp2(old - m)
+        top_ref[...] = m
+        acc_ref[...] = acc_ref[...] * jnp.concatenate([keep, keep], axis=1) + jnp.dot(
+            prob, values_of(p), preferred_element_type=jnp.float32
+        )
+
+
+def own_block(q, part_a, part_b):
+    sources, rows, width = q.shape
+    tokens = sources * rows
+    return pl.pallas_call(
+        own_block_kernel,
+        grid=(sources,),
+        in_specs=[
+            pl.BlockSpec((1, rows, width), lambda i: (i, 0, 0)),
+            pl.BlockSpec(part_a.shape, lambda i: (0, 0, 0, 0)),
+            pl.BlockSpec(part_b.shape, lambda i: (0, 0, 0, 0)),
+        ],
+        out_specs=[
+            pl.BlockSpec((rows, 2 * width), lambda i: (i, 0)),
+            pl.BlockSpec((rows, width), lambda i: (i, 0)),
+        ],
+        out_shape=[
+            jax.ShapeDtypeStruct((tokens, 2 * width), jnp.float32),
+            jax.ShapeDtypeStruct((tokens, width), jnp.float32),
+        ],
+        compiler_params=pltpu.CompilerParams(vmem_limit_bytes=VMEM_LIMIT),
+        cost_estimate=pl.CostEstimate(
+            flops=4 * tokens * tokens * width // 2, bytes_accessed=12 << 20, transcendentals=tokens * tokens // 2
+        ),
+        name="own_block",
+    )(q, part_a, part_b)
+
+
+def fold_chunk(q, kv_ref, count, acc, old):
+    scale = HD ** (-0.5) * LOG2E
+    sources, _, rows, width = kv_ref.shape
+    k = kv_ref[:, 0].reshape(sources * rows, width)
+    v = kv_ref[:, 1].reshape(sources * rows, width)
+    s = dot_t(q, k) * scale
+    m = jnp.maximum(old, jnp.max(s, axis=1, keepdims=True))
+    prob = jnp.exp2(s - m[:, :1]).astype(jnp.bfloat16)
+    keep = jnp.exp2(old - m)
+    acc = acc * jnp.concatenate([keep, keep], axis=1) + count * jnp.dot(
+        prob, with_ones(v), preferred_element_type=jnp.float32
+    )
+    return acc, m
+
+
+def chunk_kernel(meta_ref, q_ref, kv_ref, acc_in, top_in, acc_out, top_out):
+    count = meta_ref[0]
+
+    @pl.when(count > 0)
+    def _():
+        acc_out[...], top_out[...] = fold_chunk(
+            q_ref[...], kv_ref, count.astype(jnp.float32), acc_in[...], top_in[...]
+        )
+
+    @pl.when(count == 0)
+    def _():
+        acc_out[...] = acc_in[...]
+        top_out[...] = top_in[...]
+
+
+def chunk_cost(tokens, keys, width):
+    return pl.CostEstimate(
+        flops=4 * tokens * keys * width, bytes_accessed=12 << 20, transcendentals=tokens * keys
+    )
+
+
+def fold(meta, q, kv, acc, top, rows=QROWS):
+    tokens, width = q.shape
+    keys = kv.shape[0] * kv.shape[2]
+    return pl.pallas_call(
+        chunk_kernel,
+        grid_spec=pltpu.PrefetchScalarGridSpec(
+            num_scalar_prefetch=1,
+            grid=(tokens // rows,),
+            in_specs=[
+                pl.BlockSpec((rows, width), lambda i, s: (i, 0)),
+                pl.BlockSpec(kv.shape, lambda i, s: (0, 0, 0, 0)),
+                pl.BlockSpec((rows, 2 * width), lambda i, s: (i, 0)),
+                pl.BlockSpec((rows, width), lambda i, s: (i, 0)),
+            ],
+            out_specs=[
+                pl.BlockSpec((rows, 2 * width), lambda i, s: (i, 0)),
+                pl.BlockSpec((rows, width), lambda i, s: (i, 0)),
+            ],
+        ),
+        out_shape=[
+            jax.ShapeDtypeStruct(acc.shape, jnp.float32),
+            jax.ShapeDtypeStruct(top.shape, jnp.float32),
+        ],
+        input_output_aliases={3: 0, 4: 1},
+        compiler_params=pltpu.CompilerParams(vmem_limit_bytes=VMEM_LIMIT),
+        cost_estimate=chunk_cost(tokens, keys, width),
+        name="fold_chunk",
+    )(meta, q, kv, acc, top)
+
+
+def last_kernel(meta_ref, q_ref, kv_ref, acc_in, top_in, gain_ref, out_ref):
+    count = meta_ref[0]
+
+    def finish(acc):
+        out = acc[:, :HD] / acc[:, HD:]
+        out_ref[...] = (normalize(out) * gain_ref[...]).astype(jnp.bfloat16)
+
+    @pl.when(count > 0)
+    def _():
+        acc, _ = fold_chunk(q_ref[...], kv_ref, count.astype(jnp.float32), acc_in[...], top_in[...])
+        finish(acc)
+
+    @pl.when(count == 0)
+    def _():
+        finish(acc_in[...])
+
+
+def fold_last(meta, q, kv, acc, top, gain, rows=QROWS):
+    tokens, width = q.shape
+    keys = kv.shape[0] * kv.shape[2]
+    steps = tokens // rows // 2
+    return pl.pallas_call(
+        last_kernel,
+        grid_spec=pltpu.PrefetchScalarGridSpec(
+            num_scalar_prefetch=1,
+            grid=(steps,),
+            in_specs=[
+                pl.BlockSpec((rows, width), lambda i, s: (s[1] * steps + i, 0)),
+                pl.BlockSpec(kv.shape, lambda i, s: (0, 0, 0, 0)),
+                pl.BlockSpec((rows, 2 * width), lambda i, s: (s[1] * steps + i, 0)),
+                pl.BlockSpec((rows, width), lambda i, s: (s[1] * steps + i, 0)),
+                pl.BlockSpec((1, width), lambda i, s: (0, 0)),
+            ],
+            out_specs=pl.BlockSpec((rows, width), lambda i, s: (i, 0)),
+        ),
+        out_shape=jax.ShapeDtypeStruct((tokens // 2, width), jnp.bfloat16),
+        compiler_params=pltpu.CompilerParams(vmem_limit_bytes=VMEM_LIMIT),
+        cost_estimate=chunk_cost(tokens // 2, keys, width),
+        name="fold_last",
+    )(meta, q, kv, acc, top, gain)
+
+
+def states_kernel(kv_ref, weight_ref, decay_ref, entering_ref, final_ref):
+    spans = entering_ref.shape[0]
+    state = jnp.zeros((HD, HD), jnp.float32)
+    for s in range(spans):
+        rows = pl.ds(s % SUB * CH, CH)
+        entering_ref[s] = state
+        k = kv_ref[s // SUB, 0, rows, :].astype(jnp.float32)
+        v = kv_ref[s // SUB, 1, rows, :]
+        weighted = (k * weight_ref[:, s : s + 1]).astype(jnp.bfloat16)
+        inc = lax.dot_general(
+            weighted, v, (((0,), (0,)), ((), ())), preferred_element_type=jnp.float32
+        )
+        state = decay_ref[s : s + 1, :] * state + inc
+    final_ref[...] = state
+
+
+def states(kv, weight, decay):
+    spans = decay.shape[0]
+    return pl.pallas_call(
+        states_kernel,
+        out_shape=[
+            jax.ShapeDtypeStruct((spans, HD, HD), jnp.float32),
+            jax.ShapeDtypeStruct((HD, HD), jnp.float32),
+        ],
+        compiler_params=pltpu.CompilerParams(vmem_limit_bytes=VMEM_LIMIT),
+        cost_estimate=pl.CostEstimate(flops=2 * spans * CH * HD * HD * 4, bytes_accessed=4 << 20, transcendentals=0),
+        name="span_states",
+    )(kv, weight, decay)
+
+
+def linear_kernel(q_ref, kv_ref, entering_ref, carried_ref, cum_ref, cum_t_ref, lead_ref, gain_ref, out_ref):
+    spans = entering_ref.shape[0]
+    r = lax.broadcasted_iota(jnp.int32, (CH, CH), 0)
+    c = lax.broadcasted_iota(jnp.int32, (CH, CH), 1)
+    causal = c <= r
+    for s in range(spans):
+        rows = pl.ds(s % SUB * CH, CH)
+        q = q_ref[s // SUB, rows, :]
+        k = kv_ref[s // SUB, 0, rows, :]
+        v = kv_ref[s // SUB, 1, rows, :]
+        column = cum_t_ref[:, s : s + 1]
+        gap = jnp.where(causal, column - cum_ref[s : s + 1, :], 0.0)
+        damping = jnp.where(causal, jnp.exp(gap), 0.0)
+        mixing = (dot_t(q, k) * damping).astype(jnp.bfloat16)
+        inside = jnp.dot(mixing, v, preferred_element_type=jnp.float32)
+        state = entering_ref[s] + lead_ref[s : s + 1, :] * carried_ref[...]
+        high = state.astype(jnp.bfloat16)
+        low = (state - high.astype(jnp.float32)).astype(jnp.bfloat16)
+        across = jnp.dot(q, jnp.concatenate([high, low], axis=1), preferred_element_type=jnp.float32)
+        out = inside + jnp.exp(column) * (across[:, :HD] + across[:, HD:])
+        out_ref[s * CH : (s + 1) * CH, :] = (normalize(out) * gain_ref[...]).astype(jnp.bfloat16)
+
+
+def linear(q, kv, entering, carried, cum, cum_t, lead, gain):
+    spans = cum.shape[0]
+    return pl.pallas_call(
+        linear_kernel,
+        out_shape=jax.ShapeDtypeStruct((spans * CH, HD), jnp.bfloat16),
+        compiler_params=pltpu.CompilerParams(vmem_limit_bytes=VMEM_LIMIT),
+        cost_estimate=pl.CostEstimate(flops=2 * spans * CH * HD * HD * 6, bytes_accessed=6 << 20, transcendentals=0),
+        name="linear_heads",
+    )(q, kv, entering, carried, cum, cum_t, lead, gain)
+
+
+def paired_device(queries, keys, values, log_decay, selection, out_gain):
+    plane = ("x", "y", "c")
+    z, x = lax.axis_index("z"), lax.axis_index("x")
+    tokens = queries.shape[0]
+    half = tokens // 2
+    order = [4 * y + 2 * c + xx for xx in range(2) for y in range(2) for c in range(2)]
+
+    def columns(a, kind, start, stop):
+        return [a[start:stop, (2 * j + kind) * HD : (2 * j + kind + 1) * HD] for j in order]
+
+    def to_heads(parts):
+        return lax.all_to_all(parts, plane, 0, 0, tiled=True)
+
+    def pair_up(kind, start, stop):
+        return jnp.stack(
+            [jnp.stack(t) for t in zip(columns(keys, kind, start, stop), columns(values, kind, start, stop))]
+        )
+
+    part_a = to_heads(pair_up(1, 0, half))
+    part_b = to_heads(pair_up(1, half, tokens))
+    q_att = to_heads(jnp.stack(columns(queries, 1, 0, tokens)))
+    kv_lin = to_heads(pair_up(0, 0, tokens))
+    q_lin = to_heads(jnp.stack(columns(queries, 0, 0, tokens)))
+
+    others = selection[:, 1:]
+    rows_of = jnp.arange(selection.shape[0])
+
+    def count(i, b):
+        return jnp.sum((others[i] == b) & (others[i] != i)).astype(jnp.int32)
+
+    two, one = count(3, 2) > 0, count(3, 1) > 0
+    both = two & one
+    c10, c20, c21 = count(1, 0), count(2, 0), count(2, 1)
+    c30, c31, c32 = count(3, 0), count(3, 1), count(3, 2)
+    none = jnp.int32(0)
+    uses = jnp.stack(
+        [
+            jnp.stack([none, none, none, none, none]),
+            jnp.stack([c10, c10, none, none, none]),
+            jnp.stack([c21, c21, c20, c20, none]),
+            jnp.stack(
+                [
+                    c32,
+                    jnp.where(two, c32, c31),
+                    c31,
+                    jnp.where(both, c31, c30),
+                    jnp.where(both, none, c30),
+                ]
+            ),
+        ]
+    )
+    mine = lax.dynamic_index_in_dim(uses, z, 0, False)
+
+    sender = z == 2
+    up = [(0, 1), (1, 2), (2, 3)]
+    r1 = lax.ppermute(part_a, "z", up)
+    r2 = lax.ppermute(jnp.where(sender & ~two, r1, part_b), "z", up)
+    r3 = lax.ppermute(jnp.where(sender & ~two, r2, r1), "z", up[1:])
+    r4 = lax.ppermute(jnp.where(sender & ~both, r3, r2), "z", up[1:])
+    r5 = lax.ppermute(r4, "z", up[2:])
+
+    gain = lax.dynamic_slice_in_dim(out_gain, x * 2 * HD, 2 * HD).reshape(2, 1, HD)
+    acc, top = own_block(q_att, part_a, part_b)
+    q_flat = q_att.reshape(-1, HD)
+    for step, kv in enumerate((r1, r2, r3, r4)):
+        acc, top = fold(mine[step : step + 1], q_flat, kv, acc, top)
+
+    swap = [(0, 1), (1, 0)]
+    own_decay = lax.dynamic_index_in_dim(log_decay, x, 1, False)
+    sent_decay = lax.dynamic_index_in_dim(log_decay, 1 - x, 1, False)
+    got_decay = lax.ppermute(sent_decay, "x", swap)
+    decays = jnp.where(x == 0, jnp.stack([own_decay, got_decay]), jnp.stack([got_decay, own_decay]))
+    cum = jnp.cumsum(decays.reshape(-1, CH), axis=1)
+    ending = cum[:, -1]
+    spans = cum.shape[0]
+    weight = jnp.exp(ending[:, None] - cum).T
+    decay = jnp.broadcast_to(jnp.exp(ending)[:, None], (spans, HD))
+    lead = jnp.broadcast_to(jnp.exp(jnp.cumsum(ending) - ending)[:, None], (spans, HD))
+    entering, final = states(kv_lin, weight, decay)
+    whole = jnp.exp(jnp.sum(ending))
+    carried = jnp.zeros_like(final)
+    for _ in range(3):
+        carried = lax.ppermute(whole * carried + final, "z", up)
+    lin = linear(q_lin, kv_lin, entering, carried, cum, cum.T, lead, gain[0])
+    rows = lin.shape[0] // 2
+    lin_own = lax.dynamic_slice_in_dim(lin, x * rows, rows)
+    lin_got = lax.ppermute(lax.dynamic_slice_in_dim(lin, (1 - x) * rows, rows), "x", swap)
+
+    away = fold_last(jnp.stack([mine[4], 1 - x]), q_flat, r5, acc, top, gain[1])
+    att_got = lax.ppermute(away, "x", swap)
+    att_own = fold_last(jnp.stack([mine[4], x]), q_flat, r5, acc, top, gain[1])
+    return jnp.where(
+        x == 0,
+        jnp.concatenate([lin_own, att_own, lin_got, att_got], axis=1),
+        jnp.concatenate([lin_got, att_got, lin_own, att_own], axis=1),
+    )
+
+
 def solution(mesh):
+    args = (P(("seq", "head"), None),) * 3 + (P("seq", "head"), P(), P("head"))
+    if mesh.shape["seq"] == 8 and mesh.shape["head"] == 4:
+        fine = jax.sharding.Mesh(mesh.devices.reshape(4, 2, 2, 2), ("z", "x", "y", "c"))
+        everywhere = P(("z", "x", "y", "c"), None)
+        return jax.shard_map(
+            paired_device,
+            mesh=fine,
+            in_specs=(everywhere,) * 3 + (P(("z", "x"), ("y", "c")), P(), P(("y", "c"))),
+            out_specs=P(("z", "x"), ("y", "c")),
+            check_vma=False,
+        )
     return jax.shard_map(
-        per_device,
-        mesh=mesh,
-        in_specs=(
-            P(("seq", "head"), None),
-            P(("seq", "head"), None),
-            P(("seq", "head"), None),
-            P("seq", "head"),
-            P(),
-            P("head"),
-        ),
-        out_specs=P("seq", "head"),
-        check_vma=False,
-    )
+        per_device, mesh=mesh, in_specs=args, out_specs=P("seq", "head"), check_vma=False
+    )

time: 874 us -> 329 us (0.38)
  matrix products: 194 us -> 0 us
  Pallas kernels: 0 us -> 160 us
  waiting for transfers between devices: 181 us -> 49.2 us
  blocking collectives: 130 us -> 0 us
  other arithmetic: 158 us -> 36.3 us
  local copies, waits for them, and re-layouts: 151 us -> 30.7 us
  between operations: 14.4 us -> 5.38 us
    dot_general x28 -> x0, matrix products: 194 us -> none  [the longest x12 125 us: tile_step(): jnp.einsum('lij,jld->ild', probs, value_tile, preferred_element_type=jnp....]
    all_to_all x7 -> x5, waiting for transfers between devices: 181 us -> 3.5 us  [to_heads(): return lax.all_to_all(parts, plane, 0, 0, tiled=True)]
    pallas_call x0 -> x9, Pallas kernels: none -> 160 us  [the longest x4 104 us: fold(): pl.pallas_call(chunk_kernel, grid_spec=pltpu.PrefetchScalarGridSpec(num_s...]
    unnamed x1 -> x0, blocking collectives: 130 us -> none
    while x37 -> x0, local copies, waits for them, and re-layouts: 70.7 us -> none
    reduce_sum x14 -> x1, other arithmetic: 55.3 us -> 0.85 us  [count(): return jnp.sum((others[i] == b) & (others[i] != i)).astype(jnp.int32)]
    ppermute x0 -> x11, waiting for transfers between devices: none -> 45.7 us  [the longest x1 15.5 us: paired_device(): r2 = lax.ppermute(jnp.where(sender & ~two, r1, part_b), 'z', up)]
    select_n x16 -> x5, other arithmetic: 38.1 us -> 8.91 us  [the longest x1 2.71 us: paired_device(): r2 = lax.ppermute(jnp.where(sender & ~two, r1, part_b), 'z', up)]
  transfers between devices with their start and end apart: 8 -> 16, of which waited for: 6 -> 5; matrix products, arithmetic and copies ran while one was open for 15% -> 16% of each run, Pallas kernels for 0% -> 49%
where the time goes in v1:
time: 329 us; the launch traced here: 327 us
  Pallas kernels  160 us (49%)
  waiting for transfers between devices  49.2 us (15%)
  starting transfers between devices  45 us (14%)
  other arithmetic  36.3 us (11%)
  local copies, waits for them, and re-layouts  30.7 us (9%)
  between operations  5.38 us (2%)
    pallas_call x4, Pallas kernels, fold(): pl.pallas_call(chunk_kernel, grid_spec=pltpu.PrefetchScalarGridSpec(num_s...  104 us
    pallas_call x1, Pallas kernels, own_block(): pl.pallas_call(own_block_kernel, grid=(sources,), in_specs=[pl.BlockSpec(...  42.2 us
    unnamed x21, other arithmetic  20.6 us
    all_to_all x5, starting transfers between devices, to_heads(): return lax.all_to_all(parts, plane, 0, 0, tiled=True)  19.3 us
    ppermute x1, waiting for transfers between devices, paired_device(): r2 = lax.ppermute(jnp.where(sender & ~two, r1, part_b), 'z', up)  15.5 us
    unnamed x48, local copies, waits for them, and re-layouts  15.3 us
    ppermute x3, waiting for transfers between devices, paired_device(): carried = lax.ppermute(whole * carried + final, 'z', up)  12.5 us
    ppermute x1, waiting for transfers between devices, paired_device(): att_got = lax.ppermute(away, 'x', swap)  9.19 us
  transfers between devices with their start and end apart: 16, of which 5 were waited for; matrix products, arithmetic and copies ran while one was open for 16% of the time, Pallas kernels for 49%

profile of v1, /device:TPU:16, one launch (start us, length us, event | category | flops | bytes accessed | tf_op | source)
XLA Modules:
  0.0 326.9 jit_solution(12423764417227076613)
XLA Ops:
  8.5 4.2 %all-to-all-start.3 = ((bf16[8,2,256,128]{3,2,1,0:T(8,128)(2,1)}), bf16[8,2,256,128]{3,2,1,0:T(8,128)(2,1)}, u32[]{:S(2)}, u32[]{:S(2)}) async-start(bf16[8,2,256,128]{3,2,1,0:T(8,128)(2,1)} %fusion.15), calls=%async_computation.3 | async-start | bytes 2097152 | tf_op jit(solution)/shard_map/all_to_all | solution.py:454
  23.6 2.8 stack.476
  46.8 3.6 %all-to-all-start.4 = ((bf16[8,2,256,128]{3,2,1,0:T(8,128)(2,1)}), bf16[8,2,256,128]{3,2,1,0:T(8,128)(2,1)S(1)}, u32[]{:S(2)}, u32[]{:S(2)}) async-start(bf16[8,2,256,128]{3,2,1,0:T(8,128)(2,1)} %fusion.23), calls=%async_computation.4 | async-start | bytes 2097152 | tf_op jit(solution)/shard_map/all_to_all | solution.py:454
  50.4 3.5 %collective-permute-start.4 = (bf16[8,2,256,128]{3,2,1,0:T(8,128)(2,1)}, bf16[8,2,256,128]{3,2,1,0:T(8,128)(2,1)S(1)}, u32[]{:S(2)}, u32[]{:S(2)}) collective-permute-start(bf16[8,2,256,128]{3,2,1,0:T(8,128)(2,1)} %all-to-all-done.3.a_ref), channel_id=1, source_target_pairs={{0,8},{8,16},{16,24},{1,9},{9,17},{17,25},{2,10},{10,18},{18,26},{... | collective-permute-start | bytes 3145736 | tf_op jit(solution)/shard_map/ppermute | solution.py:498
  61.2 3.5 %all-to-all-done.4.b_ref = bf16[8,2,256,128]{3,2,1,0:T(8,128)(2,1)S(1)} async-done(((bf16[8,2,256,128]{3,2,1,0:T(8,128)(2,1)}), bf16[8,2,256,128]{3,2,1,0:T(8,128)(2,1)S(1)}, u32[]{:S(2)}, u32[]{:S(2)}) %all-to-all-start.4) | async-done | bytes 1048608 | tf_op jit(solution)/shard_map/all_to_all | solution.py:454
  65.8 3.6 %all-to-all-start.1 = ((bf16[8,2,512,128]{3,2,1,0:T(8,128)(2,1)}), bf16[8,2,512,128]{3,2,1,0:T(8,128)(2,1)S(1)}, u32[]{:S(2)}, u32[]{:S(2)}) async-start(bf16[8,2,512,128]{3,2,1,0:T(8,128)(2,1)} %fusion.7), calls=%async_computation.1 | async-start | bytes 4194304 | tf_op jit(solution)/shard_map/all_to_all | solution.py:454
  69.4 8.5 %collective-permute-done.4.kv_ref = bf16[8,2,256,128]{3,2,1,0:T(8,128)(2,1)S(1)} collective-permute-done((bf16[8,2,256,128]{3,2,1,0:T(8,128)(2,1)}, bf16[8,2,256,128]{3,2,1,0:T(8,128)(2,1)S(1)}, u32[]{:S(2)}, u32[]{:S(2)}) %collective-permute-start.4) | collective-permute-done | bytes 1048608 | tf_op jit(solution)/shard_map/ppermute | solution.py:498
  77.9 2.7 broadcast_select_fusion.1
  80.6 3.5 %collective-permute-start.5 = (bf16[8,2,256,128]{3,2,1,0:T(8,128)(2,1)}, bf16[8,2,256,128]{3,2,1,0:T(8,128)(2,1)}, u32[]{:S(2)}, u32[]{:S(2)}) collective-permute-start(bf16[8,2,256,128]{3,2,1,0:T(8,128)(2,1)} %broadcast_select_fusion.1), channel_id=1, source_target_pairs={{0,8},{8,16},{16,24},{1,9},{9,17},{17,25},{2,10},{10,18},{18,26},{... | collective-permute-start | bytes 3145736 | tf_op jit(solution)/shard_map/ppermute | solution.py:499
  92.0 15.5 %collective-permute-done.5.kv_ref = bf16[8,2,256,128]{3,2,1,0:T(8,128)(2,1)} collective-permute-done((bf16[8,2,256,128]{3,2,1,0:T(8,128)(2,1)}, bf16[8,2,256,128]{3,2,1,0:T(8,128)(2,1)}, u32[]{:S(2)}, u32[]{:S(2)}) %collective-permute-start.5) | collective-permute-done | bytes 1048608 | tf_op jit(solution)/shard_map/ppermute | solution.py:499
  108.6 3.5 %collective-permute-start.6 = (bf16[8,2,256,128]{3,2,1,0:T(8,128)(2,1)}, bf16[8,2,256,128]{3,2,1,0:T(8,128)(2,1)}, u32[]{:S(2)}, u32[]{:S(2)}) collective-permute-start(bf16[8,2,256,128]{3,2,1,0:T(8,128)(2,1)} %broadcast_select_fusion), channel_id=1, source_target_pairs={{8,16},{16,24},{9,17},{17,25},{10,18},{18,26},{11,19},{19,27},{12,... | collective-permute-start | bytes 3145736 | tf_op jit(solution)/shard_map/ppermute | solution.py:500
  114.9 3.6 %all-to-all-start.2 = ((bf16[8,512,128]{2,1,0:T(8,128)(2,1)}), bf16[8,512,128]{2,1,0:T(8,128)(2,1)S(1)}, u32[]{:S(2)}, u32[]{:S(2)}) async-start(bf16[8,512,128]{2,1,0:T(8,128)(2,1)} %bitcast_dynamic-update-slice_fusion), calls=%async_computation.2 | async-start | bytes 2097152 | tf_op jit(solution)/shard_map/all_to_all | solution.py:454
  123.4 12.5 %collective-permute-done.1 = f32[128,128]{1,0:T(8,128)S(1)} collective-permute-done((f32[128,128]{1,0:T(8,128)S(1)}, f32[128,128]{1,0:T(8,128)S(1)}, u32[]{:S(2)}, u32[]{:S(2)}) %collective-permute-start.1) | collective-permute-done | bytes 65568 | tf_op jit(solution)/shard_map/ppermute | solution.py:525
  135.8 3.5 %collective-permute-start.2 = (f32[128,128]{1,0:T(8,128)S(1)}, f32[128,128]{1,0:T(8,128)S(1)}, u32[]{:S(2)}, u32[]{:S(2)}) collective-permute-start(f32[128,128]{1,0:T(8,128)S(1)} %multiply_add_fusion.1), channel_id=1, source_target_pairs={{0,8},{8,16},{16,24},{1,9},{9,17},{17,25},{2,10},{10,18},{18,26},{... | collective-permute-start | bytes 196616 | tf_op jit(solution)/shard_map/ppermute | solution.py:525
  143.6 4.3 %all-to-all-start = ((bf16[8,512,128]{2,1,0:T(8,128)(2,1)}), bf16[8,512,128]{2,1,0:T(8,128)(2,1)}, u32[]{:S(2)}, u32[]{:S(2)}) async-start(bf16[8,512,128]{2,1,0:T(8,128)(2,1)} %get-tuple-element.55), calls=%async_computation | async-start | bytes 2097152 | tf_op jit(solution)/shard_map/all_to_all | solution.py:454
  149.1 42.2 %own_block.1 = (f32[4096,256]{1,0:T(8,128)}, f32[4096,128]{1,0:T(8,128)S(1)}) custom-call(bf16[8,512,128]{2,1,0:T(8,128)(2,1)S(1)} %all-to-all-done.2.q_ref, bf16[8,2,256,128]{3,2,1,0:T(8,128)(2,1)} %all-to-all-done.3.a_ref, bf16[8,2,256,128]{3,2,1,0:T(8,128)(2,1)S(1)} %copy-done.5), custom_call_target="tpu_custom_call" | custom-call | flops 4294967296 | bytes 12582912 | tf_op jit(solution)/shard_map/own_block/pallas_call | solution.py:247
  193.4 25.7 %fold_chunk.4 = (f32[4096,256]{1,0:T(8,128)}, f32[4096,128]{1,0:T(8,128)S(1)}) custom-call(s32[1]{0:T(128)} %bitcast.110.meta_ref, bf16[4096,128]{1,0:T(8,128)(2,1)S(1)} %bitcast.255, bf16[8,2,256,128]{3,2,1,0:T(8,128)(2,1)S(1)} %copy-done.3, f32[4096,256]{1,0:T(8,128)} %get-tuple-element.19.acc_in, ...), custom_call_target="tpu_custom_call", output_to_operand_aliasing={{0}: (3, {}), {1}: (4, {})} | custom-call | flops 4294967296 | bytes 12582912 | tf_op jit(solution)/shard_map/fold_chunk/pallas_call | solution.py:310
  220.5 5.5 %linear_heads.1 = bf16[4096,128]{1,0:T(8,128)(2,1)S(1)} custom-call(bf16[8,512,128]{2,1,0:T(8,128)(2,1)} %all-to-all-done.q_ref, bf16[8,2,512,128]{3,2,1,0:T(8,128)(2,1)S(1)} %all-to-all-done.1.kv_ref, f32[32,128,128]{2,1,0:T(8,128)} %copy-done.6, f32[128,128]{1,0:T(8,128)S(1)} %collective-permute-done.3.carried_ref, ...), custom_call_target="tpu_custom_call" | custom-call | flops 805306368 | bytes 6291456 | tf_op jit(solution)/shard_map/linear_heads/pallas_call | solution.py:434
  229.7 26.1 %fold_chunk.5 = (f32[4096,256]{1,0:T(8,128)}, f32[4096,128]{1,0:T(8,128)S(1)}) custom-call(s32[1]{0:T(128)} %bitcast.109.meta_ref, bf16[4096,128]{1,0:T(8,128)(2,1)S(1)} %bitcast.256, bf16[8,2,256,128]{3,2,1,0:T(8,128)(2,1)} %collective-permute-done.5.kv_ref, f32[4096,256]{1,0:T(8,128)} %get-tuple-element.21.acc_in, ...), custom_call_target="tpu_custom_call", output_to_operand_aliasing={{0}: (3, {}), {1}: (4, {})} | custom-call | flops 4294967296 | bytes 12582912 | tf_op jit(solution)/shard_map/fold_chunk/pallas_call | solution.py:310
  255.7 26.2 %fold_chunk.6 = (f32[4096,256]{1,0:T(8,128)}, f32[4096,128]{1,0:T(8,128)S(1)}) custom-call(s32[1]{0:T(128)} %bitcast.108.meta_ref, bf16[4096,128]{1,0:T(8,128)(2,1)S(1)} %bitcast.257, bf16[8,2,256,128]{3,2,1,0:T(8,128)(2,1)} %collective-permute-done.6.kv_ref, f32[4096,256]{1,0:T(8,128)} %get-tuple-element.23.acc_in, ...), custom_call_target="tpu_custom_call", output_to_operand_aliasing={{0}: (3, {}), {1}: (4, {})} | custom-call | flops 4294967296 | bytes 12582912 | tf_op jit(solution)/shard_map/fold_chunk/pallas_call | solution.py:310
  281.9 26.1 %fold_chunk.7 = (f32[4096,256]{1,0:T(8,128)}, f32[4096,128]{1,0:T(8,128)S(1)}) custom-call(s32[1]{0:T(128)} %bitcast.107.meta_ref, bf16[4096,128]{1,0:T(8,128)(2,1)S(1)} %bitcast.258, bf16[8,2,256,128]{3,2,1,0:T(8,128)(2,1)} %collective-permute-done.7.kv_ref, f32[4096,256]{1,0:T(8,128)} %get-tuple-element.25.acc_in, ...), custom_call_target="tpu_custom_call", output_to_operand_aliasing={{0}: (3, {}), {1}: (4, {})} | custom-call | flops 4294967296 | bytes 12582912 | tf_op jit(solution)/shard_map/fold_chunk/pallas_call | solution.py:310
  308.0 3.2 fold_last.3
  312.3 3.5 %fold_last.2 = bf16[2048,128]{1,0:T(8,128)(2,1)S(1)} custom-call(s32[2]{0:T(128)S(1)} %pad_add_fusion.1.meta_ref, bf16[4096,128]{1,0:T(8,128)(2,1)S(1)} %bitcast.260, bf16[8,2,256,128]{3,2,1,0:T(8,128)(2,1)S(1)} %collective-permute-done.8.kv_ref, f32[4096,256]{1,0:T(8,128)} %get-tuple-element.27.acc_in, f32[4096,128]{1,0:T(8,128)S(1)} %get-tuple-element.28.top_in, ...), custom_call_target="tpu_custom_call" | custom-call | flops 2147483648 | bytes 12582912 | tf_op jit(solution)/shard_map/fold_last/pallas_call | solution.py:358
  315.8 9.2 %collective-permute-done.10 = bf16[2048,128]{1,0:T(8,128)(2,1)S(1)} collective-permute-done((bf16[2048,128]{1,0:T(8,128)(2,1)S(1)}, bf16[2048,128]{1,0:T(8,128)(2,1)S(1)}, u32[]{:S(2)}, u32[]{:S(2)}) %collective-permute-start.10) | collective-permute-done | bytes 524320 | tf_op jit(solution)/shard_map/ppermute | solution.py:532
  (126 shorter events, 75.3 us)
Async XLA Ops:
  8.5 38.3 %all-to-all-start.3 = ((bf16[8,2,256,128]{3,2,1,0:T(8,128)(2,1)}), bf16[8,2,256,128]{3,2,1,0:T(8,128)(2,1)}, u32[]{:S(2)}, u32[]{:S(2)}) async-start(bf16[8,2,256,128]{3,2,1,0:T(8,128)(2,1)} %fusion.15), calls=%async_computation.3 | async-start | bytes 2097152 | tf_op jit(solution)/shard_map/all_to_all | solution.py:454
  13.4 98.7 %collective-permute-start = (f32[2048]{0:T(1024)}, f32[2048]{0:T(1024)}, u32[]{:S(2)}, u32[]{:S(2)}) collective-permute-start(f32[2048]{0:T(1024)} %bitcast.33), channel_id=1, source_target_pairs={{0,4},{4,0},{1,5},{5,1},{2,6},{6,2},{3,7},{7,3},{8,12},{12,8},{9,1... | collective-permute-start | bytes 24584 | tf_op jit(solution)/shard_map/ppermute | solution.py:513
  22.9 14.2 %copy-start.11 = (bf16[1,256,128]{2,1,0:T(8,128)(2,1)S(1)}, bf16[1,256,128]{2,1,0:T(8,128)(2,1)}, u32[]{:S(2)}) copy-start(bf16[1,256,128]{2,1,0:T(8,128)(2,1)} %get-tuple-element.67) | copy-start | bytes 196612
  22.9 14.2 %copy-start.13 = (bf16[1,256,128]{2,1,0:T(8,128)(2,1)S(1)}, bf16[1,256,128]{2,1,0:T(8,128)(2,1)}, u32[]{:S(2)}) copy-start(bf16[1,256,128]{2,1,0:T(8,128)(2,1)} %get-tuple-element.83) | copy-start | bytes 196612
  22.9 14.8 %copy-start.9 = (bf16[1,512,128]{2,1,0:T(8,128)(2,1)S(1)}, bf16[1,512,128]{2,1,0:T(8,128)(2,1)}, u32[]{:S(2)}) copy-start(bf16[1,512,128]{2,1,0:T(8,128)(2,1)} %get-tuple-element.53) | copy-start | bytes 393220
  22.9 14.8 %copy-start.10 = (bf16[1,512,128]{2,1,0:T(8,128)(2,1)S(1)}, bf16[1,512,128]{2,1,0:T(8,128)(2,1)}, u32[]{:S(2)}) copy-start(bf16[1,512,128]{2,1,0:T(8,128)(2,1)} %get-tuple-element.111) | copy-start | bytes 393220
  40.6 14.9 %copy-start.19 = (f32[512]{0:T(512)S(1)}, f32[512]{0:T(512)}, u32[]{:S(2)}) copy-start(f32[512]{0:T(512)} %param.11) | copy-start | bytes 6148
  46.8 17.9 %all-to-all-start.4 = ((bf16[8,2,256,128]{3,2,1,0:T(8,128)(2,1)}), bf16[8,2,256,128]{3,2,1,0:T(8,128)(2,1)S(1)}, u32[]{:S(2)}, u32[]{:S(2)}) async-start(bf16[8,2,256,128]{3,2,1,0:T(8,128)(2,1)} %fusion.23), calls=%async_computation.4 | async-start | bytes 2097152 | tf_op jit(solution)/shard_map/all_to_all | solution.py:454
  50.4 27.6 %collective-permute-start.4 = (bf16[8,2,256,128]{3,2,1,0:T(8,128)(2,1)}, bf16[8,2,256,128]{3,2,1,0:T(8,128)(2,1)S(1)}, u32[]{:S(2)}, u32[]{:S(2)}) collective-permute-start(bf16[8,2,256,128]{3,2,1,0:T(8,128)(2,1)} %all-to-all-done.3.a_ref), channel_id=1, source_target_pairs={{0,8},{8,16},{16,24},{1,9},{9,17},{17,25},{2,10},{10,18},{18,26},{... | collective-permute-start | bytes 3145736 | tf_op jit(solution)/shard_map/ppermute | solution.py:498
  65.8 49.1 %all-to-all-start.1 = ((bf16[8,2,512,128]{3,2,1,0:T(8,128)(2,1)}), bf16[8,2,512,128]{3,2,1,0:T(8,128)(2,1)S(1)}, u32[]{:S(2)}, u32[]{:S(2)}) async-start(bf16[8,2,512,128]{3,2,1,0:T(8,128)(2,1)} %fusion.7), calls=%async_computation.1 | async-start | bytes 4194304 | tf_op jit(solution)/shard_map/all_to_all | solution.py:454
  77.9 29.5 %copy-start.2 = (bf16[8,2,256,128]{3,2,1,0:T(8,128)(2,1)}, bf16[8,2,256,128]{3,2,1,0:T(8,128)(2,1)S(1)}, u32[]{:S(2)}) copy-start(bf16[8,2,256,128]{3,2,1,0:T(8,128)(2,1)S(1)} %collective-permute-done.4.kv_ref) | copy-start | bytes 3145732
  80.6 26.8 %collective-permute-start.5 = (bf16[8,2,256,128]{3,2,1,0:T(8,128)(2,1)}, bf16[8,2,256,128]{3,2,1,0:T(8,128)(2,1)}, u32[]{:S(2)}, u32[]{:S(2)}) collective-permute-start(bf16[8,2,256,128]{3,2,1,0:T(8,128)(2,1)} %broadcast_select_fusion.1), channel_id=1, source_target_pairs={{0,8},{8,16},{16,24},{1,9},{9,17},{17,25},{2,10},{10,18},{18,26},{... | collective-permute-start | bytes 3145736 | tf_op jit(solution)/shard_map/ppermute | solution.py:499
  108.6 30.7 %collective-permute-start.6 = (bf16[8,2,256,128]{3,2,1,0:T(8,128)(2,1)}, bf16[8,2,256,128]{3,2,1,0:T(8,128)(2,1)}, u32[]{:S(2)}, u32[]{:S(2)}) collective-permute-start(bf16[8,2,256,128]{3,2,1,0:T(8,128)(2,1)} %broadcast_select_fusion), channel_id=1, source_target_pairs={{8,16},{16,24},{9,17},{17,25},{10,18},{18,26},{11,19},{19,27},{12,... | collective-permute-start | bytes 3145736 | tf_op jit(solution)/shard_map/ppermute | solution.py:500
  114.9 28.7 %all-to-all-start.2 = ((bf16[8,512,128]{2,1,0:T(8,128)(2,1)}), bf16[8,512,128]{2,1,0:T(8,128)(2,1)S(1)}, u32[]{:S(2)}, u32[]{:S(2)}) async-start(bf16[8,512,128]{2,1,0:T(8,128)(2,1)} %bitcast_dynamic-update-slice_fusion), calls=%async_computation.2 | async-start | bytes 2097152 | tf_op jit(solution)/shard_map/all_to_all | solution.py:454
  120.6 21.1 %copy-start.6 = (f32[32,128,128]{2,1,0:T(8,128)}, f32[32,128,128]{2,1,0:T(8,128)S(1)}, u32[]{:S(2)}) copy-start(f32[32,128,128]{2,1,0:T(8,128)S(1)} %get-tuple-element.17.entering_ref) | copy-start | bytes 6291460
  120.7 15.1 %collective-permute-start.1 = (f32[128,128]{1,0:T(8,128)S(1)}, f32[128,128]{1,0:T(8,128)S(1)}, u32[]{:S(2)}, u32[]{:S(2)}) collective-permute-start(f32[128,128]{1,0:T(8,128)S(1)} %broadcast_add_fusion), channel_id=1, source_target_pairs={{0,8},{8,16},{16,24},{1,9},{9,17},{17,25},{2,10},{10,18},{18,26},{... | collective-permute-start | bytes 196616 | tf_op jit(solution)/shard_map/ppermute | solution.py:525
  135.8 55.5 %collective-permute-start.2 = (f32[128,128]{1,0:T(8,128)S(1)}, f32[128,128]{1,0:T(8,128)S(1)}, u32[]{:S(2)}, u32[]{:S(2)}) collective-permute-start(f32[128,128]{1,0:T(8,128)S(1)} %multiply_add_fusion.1), channel_id=1, source_target_pairs={{0,8},{8,16},{16,24},{1,9},{9,17},{17,25},{2,10},{10,18},{18,26},{... | collective-permute-start | bytes 196616 | tf_op jit(solution)/shard_map/ppermute | solution.py:525
  141.7 86.4 %collective-permute-start.7 = (bf16[8,2,256,128]{3,2,1,0:T(8,128)(2,1)}, bf16[8,2,256,128]{3,2,1,0:T(8,128)(2,1)}, u32[]{:S(2)}, u32[]{:S(2)}) collective-permute-start(bf16[8,2,256,128]{3,2,1,0:T(8,128)(2,1)} %broadcast_select_fusion.2), channel_id=1, source_target_pairs={{8,16},{16,24},{9,17},{17,25},{10,18},{18,26},{11,19},{19,27},{12,... | collective-permute-start | bytes 3145736 | tf_op jit(solution)/shard_map/ppermute | solution.py:501
  143.6 76.8 %all-to-all-start = ((bf16[8,512,128]{2,1,0:T(8,128)(2,1)}), bf16[8,512,128]{2,1,0:T(8,128)(2,1)}, u32[]{:S(2)}, u32[]{:S(2)}) async-start(bf16[8,512,128]{2,1,0:T(8,128)(2,1)} %get-tuple-element.55), calls=%async_computation | async-start | bytes 2097152 | tf_op jit(solution)/shard_map/all_to_all | solution.py:454
  149.1 44.3 %copy-start.3 = (bf16[8,2,256,128]{3,2,1,0:T(8,128)(2,1)S(1)}, bf16[8,2,256,128]{3,2,1,0:T(8,128)(2,1)}, u32[]{:S(2)}) copy-start(bf16[8,2,256,128]{3,2,1,0:T(8,128)(2,1)} %copy-done.2) | copy-start | bytes 3145732
  191.3 29.2 %collective-permute-start.3 = (f32[128,128]{1,0:T(8,128)S(1)}, f32[128,128]{1,0:T(8,128)S(1)}, u32[]{:S(2)}, u32[]{:S(2)}) collective-permute-start(f32[128,128]{1,0:T(8,128)S(1)} %multiply_add_fusion), channel_id=1, source_target_pairs={{0,8},{8,16},{16,24},{1,9},{9,17},{17,25},{2,10},{10,18},{18,26},{... | collective-permute-start | bytes 196616 | tf_op jit(solution)/shard_map/ppermute | solution.py:525
  226.1 89.7 %collective-permute-start.9 = (bf16[2048,128]{1,0:T(8,128)(2,1)S(1)}, bf16[2048,128]{1,0:T(8,128)(2,1)S(1)}, u32[]{:S(2)}, u32[]{:S(2)}) collective-permute-start(bf16[2048,128]{1,0:T(8,128)(2,1)S(1)} %get-tuple-element.100), channel_id=1, source_target_pairs={{0,4},{4,0},{1,5},{5,1},{2,6},{6,2},{3,7},{7,3},{8,12},{12,8},{9,1... | collective-permute-start | bytes 1572872 | tf_op jit(solution)/shard_map/ppermute | solution.py:529
  228.1 79.9 %collective-permute-start.8 = (bf16[8,2,256,128]{3,2,1,0:T(8,128)(2,1)}, bf16[8,2,256,128]{3,2,1,0:T(8,128)(2,1)S(1)}, u32[]{:S(2)}, u32[]{:S(2)}) collective-permute-start(bf16[8,2,256,128]{3,2,1,0:T(8,128)(2,1)} %collective-permute-done.7.kv_ref), channel_id=1, source_target_pairs={{16,24},{17,25},{18,26},{19,27},{20,28},{21,29},{22,30},{23,31}} | collective-permute-start | bytes 3145736 | tf_op jit(solution)/shard_map/ppermute | solution.py:502
  311.2 13.8 %collective-permute-start.10 = (bf16[2048,128]{1,0:T(8,128)(2,1)S(1)}, bf16[2048,128]{1,0:T(8,128)(2,1)S(1)}, u32[]{:S(2)}, u32[]{:S(2)}) collective-permute-start(bf16[2048,128]{1,0:T(8,128)(2,1)S(1)} %fold_last.3), channel_id=1, source_target_pairs={{0,4},{4,0},{1,5},{5,1},{2,6},{6,2},{3,7},{7,3},{8,12},{12,8},{9,1... | collective-permute-start | bytes 1572872 | tf_op jit(solution)/shard_map/ppermute | solution.py:532
  (12 other events, 66.6 us)
